TPU v7x, 32 devices: a whole 2x2x4 slice. The times are simulated.
32 devices in a mesh: groups: 2 (over x), blk: 4 (over y, core), row: 4 (over z).
Axes of the slice: x: 2, y: 2, z: 4, core: 2. Of those that a mesh axis runs over, the one named last changes fastest.
Arguments:
- coords: float32 [3, 24576], P(None, ('groups', 'blk', 'row')), parts along dimension 1, may hold values from 0 to 1
- charges: float32 [24576], P(('groups', 'blk', 'row')), parts along dimension 0, may hold values from -1 to 1
- counts: int32 [32], P(('groups', 'blk', 'row')), parts along dimension 0, may hold values from 256 to 768, as said below
- send_slot: int32 [24576], P(('groups', 'blk', 'row')), parts along dimension 0, may hold values from 0 to 1023, as said below
- recv_index: int32 [16384], P(('groups', 'blk', 'row')), parts along dimension 0, may hold values from 0 to 1023, as said below
- wave_ints: int32 [3, 24576], P(None, 'blk'), may hold values from -36 to 36, as said below
Outputs:
- slot_forces: float32 [3, 24576], P(None, ('groups', 'blk', 'row')), parts along dimension 1
- atom_forces: float32 [3, 16384], P(None, ('groups', 'blk', 'row')), parts along dimension 1
There are 2 independent parts, one for each index of `groups`. A program takes and returns all parts, laid end to end along the dimension named above; an argument that names none is the same for every part. Nothing has to cross between parts.
Inputs may be any that keep to these rules, and one draw needn't show every extreme that they name: The counts of one system sum to 8192; the largest is 768. `send_slot`: for a live slot the value is d * 64 + r: the ion goes to k-space device d as its r-th arrival from this owner. Live values of one owner are distinct, and the ranks r to one device are 0 up to the number sent there minus one. Every device receives exactly 512 ions; some owner sends exactly 64 to some device. Slots that are not live hold arbitrary values. `recv_index`: the 512 values of device d are distinct and are exactly the arrivals s * 64 + r sent to d. `wave_ints`: each column is (h, k, l) with |h|, |k| at most 12 and l nonzero.
All inputs are finite; a program needn't handle non-finite values.
Results may differ from a plain program's by a relative error of at most 0.00007.
Values sent between devices are 32-bit elements; how exact they have to be, the bound alone decides.
A program may use at most 128 MiB of HBM per device.

v0:
```python
import functools
import math

import jax
import jax.numpy as jnp
from jax import lax
from jax.experimental import pallas as pl
from jax.experimental.pallas import tpu as pltpu
from jax.sharding import PartitionSpec as P

EWALD_BETA = 30.0
BOX_Z = 3.0
FORCE_GAIN = 400.0
HMAX = 12
LMAX = 36
SIDE = 2 * HMAX
FOLD = (2 * HMAX + 1) * SIDE
PAIRS = 640
L_ROWS = 2 * LMAX
L_TILES = L_ROWS // 8
P_TILES = PAIRS // 128
TILES = L_TILES * P_TILES
F32 = jnp.float32
BF16 = jnp.bfloat16

SIN_C = [(-1) ** n * math.pi ** (2 * n + 1) / math.factorial(2 * n + 1) for n in range(7)]
COS_C = [(-1) ** n * math.pi ** (2 * n) / math.factorial(2 * n) for n in range(8)]
NT = (((1,), (1,)), ((), ()))
NN = (((1,), (0,)), ((), ()))


def iota(shape, dim):
    return lax.broadcasted_iota(jnp.int32, shape, dim)


def horner(coefs, u):
    out = jnp.full_like(u, coefs[-1])
    for c in coefs[-2::-1]:
        out = out * u + c
    return out


def turns(mult, frac):
    high = jnp.floor(frac * 4096.0 + 0.5) * (1.0 / 4096.0)
    low = frac - high
    whole = mult * high
    r = (whole - jnp.floor(whole + 0.5)) + mult * low
    u = r * r
    s = r * horner(SIN_C, u)
    c = horner(COS_C, u)
    return 1.0 - 2.0 * s * s, 2.0 * s * c


def split2(x):
    hi = x.astype(BF16)
    return hi, (x - hi.astype(F32)).astype(BF16)


def split3(x):
    hi = x.astype(BF16)
    rest = x - hi.astype(F32)
    mid = rest.astype(BF16)
    return hi, mid, (rest - mid.astype(F32)).astype(BF16)


def mm(a, b, dims):
    return lax.dot_general(a, b, dims, preferred_element_type=F32)


def l_column():
    row = iota((L_ROWS, 1), 0)
    return (4 * (row // 8) + row % 4 + 1).astype(F32), (row % 8) < 4


def pair_rows():
    n = iota((1, PAIRS), 1)
    tall = n < FOLD
    q = n // SIDE
    h = jnp.where(tall, q - HMAX, n - FOLD - HMAX)
    k = jnp.where(tall, n - q * SIDE - HMAX, HMAX)
    return h.astype(F32), k.astype(F32)


def fill_pairs(frac_x, frac_y, table, first):
    width = frac_x.shape[1]
    lanes = pl.ds(first, width)
    mult = (iota((32, 1), 0) - HMAX).astype(F32)
    cx, sx = turns(mult, frac_x)
    cy, sy = turns(mult, frac_y)
    cyk, syk = cy[:SIDE], sy[:SIDE]

    def put(start, c, s):
        for part, value in enumerate((c, s)):
            hi, lo = split2(value)
            table[pl.ds(part * PAIRS + start, c.shape[0]), lanes] = hi
            table[pl.ds((part + 2) * PAIRS + start, c.shape[0]), lanes] = lo

    def one(i):
        a, b = cx[i : i + 1], sx[i : i + 1]
        return a * cyk - b * syk, b * cyk + a * syk

    for i in range(0, 2 * HMAX, 2):
        (c0, s0), (c1, s1) = one(i), one(i + 1)
        put(i * SIDE, jnp.concatenate([c0, c1]), jnp.concatenate([s0, s1]))
    c0, s0 = one(2 * HMAX)
    a, b = cy[SIDE : SIDE + 1], sy[SIDE : SIDE + 1]
    pad = jnp.zeros((8, width), F32)
    put(
        2 * HMAX * SIDE,
        jnp.concatenate([c0, cx * a - sx * b, pad]),
        jnp.concatenate([s0, sx * a + cx * b, pad]),
    )


def tiles_out(ref, value, count):
    for t in range(count):
        if t < TILES:
            i, j = t // P_TILES, t % P_TILES
            ref[t] = value[8 * i : 8 * i + 8, 128 * j : 128 * j + 128]
        else:
            ref[t] = jnp.zeros((8, 128), F32)


def each(count, f):
    if count <= 16:
        for o in range(1, count):
            f(o)
    else:
        pl.loop(1, count)(f)


def kernel(
    blks, rows, cap, scale,
    coords, charges, counts, send_slot, recv_index, wave,
    forces,
    table, mail, got_mail, sums, from_sib, half_sums, got_t, own, grid,
    m_s, m_r, x_s, x_r, t_s, t_r, g_s, g_r, f_s, f_r,
):
    devices = blks * rows
    chips = devices // 2
    slots = coords.shape[1]
    atoms = recv_index.shape[0]
    blk, row = lax.axis_index("blk"), lax.axis_index("row")
    me = blk * rows + row
    core = blk % 2
    chip = blk // 2 * rows + row
    share = own.shape[0]
    half = chips * share
    tile_count = 2 * half
    mine = core * half
    mesh_id = pl.DeviceIdType.MESH
    sibling = {"blk": blk + 1 - 2 * core, "row": row}

    def other(o):
        d = (me + o) % devices
        return d, {"blk": d // rows, "row": d % rows}

    def other_chip(o):
        c = (chip + o) % chips
        return c, {"blk": c // rows * 2 + core, "row": c % rows}

    def copy(src, dst, s, r, o, dev):
        return pltpu.make_async_remote_copy(
            src_ref=src, dst_ref=dst, send_sem=s.at[o], recv_sem=r.at[o],
            device_id=dev, device_id_type=mesh_id,
        )

    def mail_copy(o):
        d, dev = other(o)
        return copy(mail.at[d], got_mail.at[o], m_s, m_r, o, dev)

    def sib_copy():
        return copy(sums.at[pl.ds(half - mine, half)], from_sib, x_s, x_r, 0, sibling)

    def sums_copy(o):
        c, dev = other_chip(o)
        return copy(half_sums.at[pl.ds(c * share, share)], got_t.at[o], t_s, t_r, o, dev)

    def grid_copy(o):
        _, dev = other_chip(o)
        return copy(own, grid.at[pl.ds(mine + chip * share, share)], g_s, g_r, o, dev)

    def pass_on(o):
        c = (chip + chips - o) % chips
        place = grid.at[pl.ds(mine + c * share, share)]
        return copy(own if isinstance(o, int) and o == 0 else place, place, f_s, f_r, o, sibling)

    barrier = pltpu.get_barrier_semaphore()
    each(
        devices,
        lambda o: pl.semaphore_signal(
            barrier, inc=1, device_id=other(o)[1], device_id_type=mesh_id
        ),
    )

    live = iota((1, slots), 1) < counts[0]
    q = jnp.where(live, charges[...].reshape(1, slots), 0.0)
    target = jnp.where(live, send_slot[...].reshape(1, slots), -1)
    spots = jnp.where(target == iota((devices * cap, slots), 0), 1.0, 0.0).astype(BF16)
    entries = jnp.concatenate([coords[...], q, jnp.zeros((4, slots), F32)])
    out = sum(mm(term, spots, NT) for term in split3(entries))
    per_tile = 128 // cap
    lane_part = iota((8, 128), 1) // cap
    for d in range(devices):
        tile = out[:, 128 * (d // per_tile) : 128 * (d // per_tile) + 128]
        tile = jnp.where(lane_part == d % per_tile, tile, 0.0)
        shift = (me % per_tile - d % per_tile + per_tile) % per_tile * cap
        mail[d, share] = pltpu.roll(tile, shift, 1)[:4]
    k_local = wave.shape[1]
    part = k_local // rows
    split = part % 128 == 0 and part * rows == k_local
    w = wave[:, pl.ds(pl.multiple_of(row * part, 128), part)] if split else wave[...]
    h, k, l = w[0:1], w[1:2], w[2:3]
    sign = jnp.where(l < 0, -1, 1)
    h, k, l = h * sign, k * sign, l * sign
    if not split:
        l = jnp.where(row == 0, l, 0)
    n = jnp.where(k < HMAX, (h + HMAX) * SIDE + k + HMAX, FOLD + HMAX + h)
    l_col, is_re = l_column()
    of_l = jnp.where(l.astype(F32) == l_col, 1.0, 0.0).astype(BF16)
    of_pair = jnp.where(n == iota((PAIRS, n.shape[1]), 0), 1.0, 0.0).astype(BF16)
    times = mm(of_l, of_pair, NT)
    hf, kf = pair_rows()
    two_pi = 2.0 * math.pi
    px, py, pz = two_pi * hf, two_pi * kf, two_pi * l_col / BOX_Z
    k2 = px * px + py * py + pz * pz
    times = times * (jnp.exp(-k2 / (4.0 * EWALD_BETA * EWALD_BETA)) / k2)
    for t in range(tile_count):
        c, piece = t // half, t % half // share
        d = (piece // rows * 2 + c) * rows + piece % rows
        if t < TILES:
            i, j = t // P_TILES, t % P_TILES
            mail[d, t % share] = times[8 * i : 8 * i + 4, 128 * j : 128 * j + 128]
        else:
            mail[d, t % share] = jnp.zeros((4, 128), F32)

    fill_pairs(coords[0:1], coords[1:2], table, 0)
    pl.semaphore_wait(barrier, devices - 1)
    each(devices, lambda o: mail_copy(o).start())
    cz, sz = turns(l_col, coords[2:3])
    v1h, v1l = split2(q * jnp.where(is_re, cz, sz))
    v2h, v2l = split2(q * jnp.where(is_re, -sz, cz))
    uch, ush, ucl, usl = (table[pl.ds(i * PAIRS, PAIRS), :slots] for i in range(4))
    total = mm(v1l, uch, NT) + mm(v1h, ucl, NT) + mm(v2l, ush, NT) + mm(v2h, usl, NT)
    total = total + (mm(v1h, uch, NT) + mm(v2h, ush, NT))
    for t in range(tile_count):
        if t < TILES:
            i, j = t // P_TILES, t % P_TILES
            sums[t] = total[8 * i : 8 * i + 8, 128 * j : 128 * j + 128]
        else:
            sums[t] = jnp.zeros((8, 128), F32)
    sib_copy().start()
    sib_copy().wait_recv()
    half_sums[...] = sums[pl.ds(mine, half)] + from_sib[...]
    each(chips, lambda o: sums_copy(o).start())

    each(devices, lambda o: mail_copy(o).wait_recv())
    got_mail[0] = mail[me]
    arrived = []
    for t in range(devices // per_tile):
        tile = jnp.zeros((4, 128), F32)
        for s in range(t * per_tile, (t + 1) * per_tile):
            tile = tile + got_mail[(me - s + devices) % devices, share]
        arrived.append(tile)
    came = jnp.concatenate(arrived, axis=1)
    came = jnp.concatenate([came, jnp.zeros_like(came)])
    index = recv_index[...].reshape(1, atoms)
    picks = jnp.where(index == iota((came.shape[1], atoms), 0), 1.0, 0.0).astype(BF16)
    ions = sum(mm(term, picks, NN) for term in split3(came))
    m_own = got_mail[0, :share]
    for o in range(1, devices):
        m_own = m_own + got_mail[o, :share]

    fill_pairs(ions[0:1], ions[1:2], table, slots)
    each(chips, lambda o: sums_copy(o).wait_recv())
    got_t[0] = half_sums[pl.ds(chip * share, share)]
    piece = jnp.sum(got_t[...], axis=0) * jnp.concatenate([m_own, m_own], axis=1)
    own[...] = piece
    each(chips, lambda o: grid_copy(o).start())
    pass_on(0).start()
    grid[pl.ds(mine + chip * share, share)] = piece
    cz2, sz2 = turns(l_col, ions[2:3])
    vf = jnp.where(is_re, jnp.concatenate([sz, sz2], axis=1), jnp.concatenate([cz, cz2], axis=1))
    charge = jnp.concatenate([q, ions[3:4]], axis=1)

    def forward(o):
        grid_copy(o).wait_recv()
        pass_on(o).start()

    each(chips, forward)
    pass_on(0).wait_recv()
    each(chips, lambda o: pass_on(o).wait_recv())

    tile = lambda i, j: grid[i * P_TILES + j]
    g = jnp.concatenate(
        [jnp.concatenate([tile(i, j) for j in range(P_TILES)], axis=1) for i in range(L_TILES)]
    )
    swap = jnp.concatenate(
        [
            rows4
            for i in range(L_TILES)
            for rows4 in (g[8 * i + 4 : 8 * i + 8], g[8 * i : 8 * i + 4])
        ]
    )
    gc = jnp.where(is_re, g, -g)
    gch, gcl = split2(jnp.concatenate([gc, gc * hf, gc * kf]))
    gsh, gsl = split2(jnp.concatenate([swap, swap * hf, swap * kf]))
    x = mm(jnp.concatenate([gch, gsh] * 2, axis=1), table[...], NN)
    x = x + mm(jnp.concatenate([gcl, gsl], axis=1), table[: 2 * PAIRS], NN)
    x = x * jnp.concatenate([vf] * 3)
    fz = jnp.sum(x[:L_ROWS] * (two_pi * l_col / BOX_Z), axis=0, keepdims=True)
    fx = two_pi * jnp.sum(x[L_ROWS : 2 * L_ROWS], axis=0, keepdims=True)
    fy = two_pi * jnp.sum(x[2 * L_ROWS :], axis=0, keepdims=True)
    forces[...] = scale * charge * jnp.concatenate([fx, fy, fz])

    each(devices, lambda o: mail_copy(o).wait_send())
    sib_copy().wait_send()
    each(chips, lambda o: sums_copy(o).wait_send())
    each(chips, lambda o: grid_copy(o).wait_send())
    pass_on(0).wait_send()
    each(chips, lambda o: pass_on(o).wait_send())


def deliver(counts, forces, slot_forces, atom_forces):
    slots = slot_forces.shape[1]
    live = iota((1, slots), 1) < counts[0]
    slot_forces[...] = jnp.where(live, forces[:, :slots], 0.0)
    atom_forces[...] = forces[:, slots:]


VMEM = pl.BlockSpec(memory_space=pltpu.VMEM)
SMEM = pl.BlockSpec(memory_space=pltpu.SMEM)


def body(coords, charges, counts, send_slot, recv_index, wave_ints):
    slots = charges.shape[0]
    atoms = recv_index.shape[0]
    blks, rows = lax.axis_size("blk"), lax.axis_size("row")
    devices = blks * rows
    chips = devices // 2
    cap = 2 * atoms // devices
    share = -(-TILES // devices)
    half = chips * share
    scale = FORCE_GAIN / math.sqrt(float(atoms * devices * blks * wave_ints.shape[1]))
    shape = jax.ShapeDtypeStruct
    dma = lambda n: [pltpu.SemaphoreType.DMA((n,))] * 2
    forces = pl.pallas_call(
        functools.partial(kernel, blks, rows, cap, scale),
        out_shape=shape((3, slots + atoms), F32),
        in_specs=[VMEM, VMEM, SMEM, VMEM, VMEM, VMEM],
        out_specs=VMEM,
        scratch_shapes=[pltpu.VMEM((4 * PAIRS, slots + atoms), BF16)]
        + [
            pltpu.VMEM((devices, share + 1, 4, 128), F32),
            pltpu.VMEM((devices, share + 1, 4, 128), F32),
            pltpu.VMEM((2 * half, 8, 128), F32),
            pltpu.VMEM((half, 8, 128), F32),
            pltpu.VMEM((half, 8, 128), F32),
            pltpu.VMEM((chips, share, 8, 128), F32),
            pltpu.VMEM((share, 8, 128), F32),
            pltpu.VMEM((2 * half, 8, 128), F32),
        ]
        + dma(devices) + dma(1) + dma(chips) + dma(chips) + dma(chips),
        compiler_params=pltpu.CompilerParams(
            collective_id=0, has_side_effects=True, vmem_limit_bytes=56 * 2**20
        ),
    )(coords, charges, counts, send_slot, recv_index, wave_ints)
    return pl.pallas_call(
        deliver,
        out_shape=[shape((3, slots), F32), shape((3, atoms), F32)],
        in_specs=[SMEM, VMEM],
        out_specs=[VMEM] * 2,
    )(counts, forces)


def solution(mesh):
    ions = P(("groups", "blk", "row"))
    return jax.shard_map(
        body,
        mesh=mesh,
        in_specs=(P(None, *ions), ions, ions, ions, ions, P(None, "blk")),
        out_specs=(P(None, *ions), P(None, *ions)),
        check_vma=False,
    )
```

profile of v0, /device:TPU:1, one launch (start us, length us, event | category | flops | bytes accessed | tf_op | source)
XLA Modules:
  0.0 27.2 jit_solution(17652856698786664760)
XLA Ops:
  1.3 24.5 %shard_map.77.forces = f32[3,1280]{1,0:T(4,128)} custom-call(f32[3,768]{1,0:T(4,128)} %coords.1, f32[768]{0:T(1024)} %charges.1, s32[1]{0:T(128)S(6)} %copy.8.counts, s32[768]{0:T(1024)} %send_slot.1, s32[512]{0:T(512)} %recv_index.1, s32[3,6144]{1,0:T(4,128)} %wave.1), custom_call_target="tpu_custom_call" | custom-call | tf_op jit(solution)/shard_map/pallas_call | solution.py:347
  25.8 1.3 %shard_map.78 = (f32[3,768]{1,0:T(4,128)}, f32[3,512]{1,0:T(4,128)}) custom-call(s32[1]{0:T(128)S(6)} %copy.8.counts, f32[3,1280]{1,0:T(4,128)} %shard_map.77.forces), custom_call_target="tpu_custom_call" | custom-call | tf_op jit(solution)/shard_map/pallas_call | solution.py:368
where the time goes:
time: 27.4 us; the launch traced here: 27.2 us
  Pallas kernels  25.9 us (95%)
  between operations  1.28 us (5%)
    pallas_call x1, Pallas kernels, body(): pl.pallas_call(functools.partial(kernel, blks, rows, cap, scale), out_sha...  24.5 us
    pallas_call x1, Pallas kernels, body(): pl.pallas_call(deliver, out_shape=[shape((3, slots), F32), shape((3, atom...  1.34 us

commit v1 on v0

v1 whole, which is shorter than its diff:
```python
import functools
import math

import jax
import jax.numpy as jnp
import numpy as np
from jax import lax
from jax.experimental import pallas as pl
from jax.experimental.pallas import tpu as pltpu
from jax.sharding import PartitionSpec as P

EWALD_BETA = 30.0
BOX_Z = 3.0
FORCE_GAIN = 400.0
HMAX = 12
LMAX = 36
L_ROWS = 40
QUADS = 160
REGULAR = HMAX * HMAX
WAVES = 4 * QUADS
W_TILES = WAVES // 128
H_TILES = L_ROWS // 8 * W_TILES
T_TILES = 2 * H_TILES
F32 = jnp.float32
BF16 = jnp.bfloat16
NT = (((1,), (1,)), ((), ()))
NN = (((1,), (0,)), ((), ()))
TWO_PI = 2.0 * math.pi


def fit(f, terms):
    n = 64
    u = 0.125 + 0.125 * np.cos((2 * np.arange(n) + 1) * np.pi / (2 * n))
    c = np.polynomial.chebyshev.Chebyshev.fit(u, f(np.sqrt(u)), terms - 1, domain=[0.0, 0.25])
    return [float(v) for v in c.convert(kind=np.polynomial.Polynomial).coef]


SIN_C = fit(lambda r: np.sin(np.pi * r) / r, 5)
COS_C = fit(lambda r: np.cos(np.pi * r), 5)


def iota(shape, dim):
    return lax.broadcasted_iota(jnp.int32, shape, dim)


def horner(coefs, u):
    out = u * coefs[-1] + coefs[-2]
    for c in coefs[-3::-1]:
        out = out * u + c
    return out


def turns(mult, frac):
    t = mult * frac
    r = t - jnp.floor(t + 0.5)
    u = r * r
    s = r * horner(SIN_C, u)
    c = horner(COS_C, u)
    twice = s + s
    return 1.0 - twice * s, twice * c


def split2(x):
    hi = x.astype(BF16)
    return hi, (x - hi.astype(F32)).astype(BF16)


def split3(x):
    hi = x.astype(BF16)
    rest = x - hi.astype(F32)
    mid = rest.astype(BF16)
    return hi, mid, (rest - mid.astype(F32)).astype(BF16)


def mm(a, b, dims):
    return lax.dot_general(a, b, dims, preferred_element_type=F32)


def mm3(x, picks, dims):
    rows = x.shape[0]
    out = mm(jnp.concatenate(split3(x)), picks, dims)
    return out[:rows] + out[rows : 2 * rows] + out[2 * rows :]


def quad_of(h, k):
    even = jnp.where(k <= 8, 8 * h + k - 9, 83 + 4 * h + k)
    lone = jnp.where(h + k == 0, REGULAR + HMAX, REGULAR - 1 + h + k)
    return jnp.where((h > 0) & (k > 0), even, lone)


def lane_waves():
    lane = iota((1, WAVES), 1)
    block = (lane >> 5) & 3
    quad = ((lane >> 7) << 5) + (lane & 31)
    late = quad - 96
    h = jnp.where(quad < 96, (quad >> 3) + 1, (late >> 2) + 1)
    k = jnp.where(quad < 96, (quad & 7) + 1, (late & 3) + 9)
    lone = jnp.where(quad < REGULAR + HMAX, quad - (REGULAR - 1), 0)
    regular = quad < REGULAR
    odd = (block & 1) == 1
    h = jnp.where(regular, h, jnp.where(odd, 0, lone))
    k = jnp.where(regular, k, jnp.where(odd, lone, 0))
    return h.astype(F32), k.astype(F32), block, regular


def fill_plane(frac_x, frac_y, hi, lo):
    width = frac_x.shape[1]
    row = iota((16, 1), 0)
    mult = jnp.where(row < 12, row + 1, row - 3).astype(F32)
    cx, sx = turns(mult, frac_x)
    cy, sy = turns(mult, frac_y)
    low = iota((8, width), 0) < 4

    def two(v, i):
        a = jnp.broadcast_to(v[i : i + 1], (8, width))
        return jnp.where(low, a, jnp.broadcast_to(v[i + 1 : i + 2], (8, width)))

    def unit(u):
        if u < HMAX:
            a, b = cx[u : u + 1], sx[u : u + 1]
            c, d = cy[:8], sy[:8]
        elif u < 18:
            i = 2 * (u - HMAX)
            a, b = two(cx, i), two(sx, i)
            c, d = cy[8:], sy[8:]
        elif u == 18:
            return cx[:8], cy[:8], sx[:8], sy[:8]
        else:
            return jnp.where(low, cx[8:], 1.0), cy[8:], jnp.where(low, sx[8:], 0.0), sy[8:]
        return a * c, b * d, b * c, a * d

    for t in range(W_TILES):
        units = [unit(4 * t + i) for i in range(4)]
        for block in range(4):
            value = jnp.concatenate([v[block] for v in units])
            place = pl.ds(128 * t + 32 * block, 32)
            hi[place, :], lo[place, :] = split2(value)


def column(frac_z, gain=None):
    c, s = turns((iota((8, 1), 0) + 1).astype(F32), frac_z)
    c8, s8 = c[7:8], s[7:8]
    if gain is not None:
        c, s = c * gain, s * gain
    cs, ss = [c], [s]
    for _ in range(L_ROWS // 8 - 1):
        c, s = c * c8 - s * s8, s * c8 + c * s8
        cs.append(c)
        ss.append(s)
    return jnp.concatenate(cs + ss)


def sums_of(v, hi, lo):
    vh, vl = split2(v)
    out = mm(jnp.concatenate([vh, vl]), hi, NT)
    return out[: 2 * L_ROWS] + out[2 * L_ROWS :] + mm(vh, lo, NT)


def each(count, f):
    if count <= 16:
        for o in range(1, count):
            f(o)
    else:
        pl.loop(1, count)(f)


def kernel(
    blks, rows, cap, scale,
    coords_in, charges_in, counts_in, send_in, recv_in, wave_in,
    forces,
    coords, charges, counts, send_slot, recv_index, wave,
    table, even, odd, ion, got_ion, mail, got_mail,
    hist, hist_sib, hist_chip, got_hist, acc, sums, from_sib,
    in_s, i_s, i_r, m_s, m_r, h_s, h_r, y_s, y_r, x_s, x_r,
):
    devices = blks * rows
    chips = devices // 2
    ys = blks // 2
    slots = coords.shape[1]
    atoms = recv_index.shape[0]
    both = slots + atoms
    blk, row = lax.axis_index("blk"), lax.axis_index("row")
    core = lax.rem(blk, 2)
    y = lax.div(blk, 2)
    me = blk * rows + row
    mesh_id = pl.DeviceIdType.MESH
    sibling = {"blk": blk + 1 - 2 * core, "row": row}

    loads = [
        pltpu.make_async_copy(src, dst, in_s.at[i])
        for i, (src, dst) in enumerate(
            (
                (coords_in, coords), (charges_in, charges), (counts_in, counts),
                (send_in, send_slot), (wave_in, wave), (recv_in, recv_index),
            )
        )
    ]
    for load in loads:
        load.start()

    blk_at = [lax.rem(blk + i, blks) for i in range(blks)]
    row_at = [lax.rem(row + i, rows) for i in range(rows)]

    def other(o):
        if isinstance(o, int):
            return {"blk": blk_at[o // rows], "row": row_at[o % rows]}
        return {"blk": lax.rem(blk + lax.div(o, rows), blks), "row": lax.rem(row + lax.rem(o, rows), rows)}

    def other_chip(o):
        if isinstance(o, int):
            return {"blk": blk_at[2 * (o // rows)], "row": row_at[o % rows]}
        return other(2 * rows * lax.div(o, rows) + lax.rem(o, rows))

    def copy(src, dst, s, r, o, dev):
        return pltpu.make_async_remote_copy(
            src_ref=src, dst_ref=dst, send_sem=s.at[o], recv_sem=r.at[o],
            device_id=dev, device_id_type=mesh_id,
        )

    def ion_copy(o):
        return copy(ion, got_ion.at[o], i_s, i_r, o, other_chip(o))

    def mail_copy(o):
        dev = other(o)
        return copy(mail.at[dev["blk"] * rows + dev["row"]], got_mail.at[o], m_s, m_r, o, dev)

    def hist_sib_copy():
        return copy(hist, hist_sib, h_s, h_r, 0, sibling)

    def hist_copy(o):
        return copy(hist_chip, got_hist.at[o], y_s, y_r, o, other_chip(o * rows))

    def sums_copy():
        return copy(sums, from_sib, x_s, x_r, 0, sibling)

    barrier = pltpu.get_barrier_semaphore()
    each(
        devices,
        lambda o: pl.semaphore_signal(
            barrier, inc=1, device_id=other(o), device_id_type=mesh_id
        ),
    )

    for load in loads[:3]:
        load.wait()
    live = iota((1, slots), 1) < jnp.broadcast_to(counts[...].reshape(1, 1), (1, slots))
    q = jnp.where(live, charges[...].reshape(1, slots), 0.0)
    ion[0:3] = coords[...]
    ion[3:4] = q
    pl.semaphore_wait(barrier, devices - 1)
    each(chips, lambda o: ion_copy(o).start())

    loads[3].wait()
    target = jnp.where(live, send_slot[...].reshape(1, slots), -1)
    spots = jnp.where(target == iota((devices * cap, slots), 0), 1.0, 0.0).astype(BF16)
    entries = jnp.concatenate([coords[...], q, jnp.zeros((4, slots), F32)])
    out = mm3(entries, spots, NT)
    per_tile = 128 // cap
    lane_part = iota((8, 128), 1) // cap
    for d in range(devices):
        tile = out[:, 128 * (d // per_tile) : 128 * (d // per_tile) + 128]
        tile = jnp.where(lane_part == d % per_tile, tile, 0.0)
        shift = (me % per_tile - d % per_tile + per_tile) % per_tile * cap
        mail[d] = pltpu.roll(tile, shift, 1)[:4]
    each(devices, lambda o: mail_copy(o).start())

    loads[4].wait()
    k_local = wave.shape[1]
    part = 1536 if k_local % 1536 == 0 else k_local
    found = None
    for first in range(0, k_local, part):
        w = wave[:, first : first + part]
        h, k, l = w[0:1], w[1:2], w[2:3]
        flip = l < 0
        s1 = jnp.where((h < 0) ^ flip, -1.0, 1.0)
        s2 = jnp.where((k < 0) ^ flip, -1.0, 1.0)
        h, k, l = jnp.abs(h), jnp.abs(k), jnp.abs(l)
        lone_k = (h == 0) & (k > 0)
        s1 = jnp.where(h > 0, s1, 0.0)
        s2 = jnp.where(k > 0, s2, 0.0)
        signs = (
            jnp.where(lone_k, 0.0, 1.0),
            jnp.where(lone_k, 1.0, s1 * s2),
            s1,
            jnp.where(lone_k, -s2, jnp.where(h > 0, s2, 0.0)),
        )
        of_l = l == iota((L_ROWS, part), 0) + 1
        left = jnp.concatenate([jnp.where(of_l, s, 0.0).astype(BF16) for s in signs])
        right = jnp.where(quad_of(h, k) == iota((QUADS, part), 0), 1.0, 0.0).astype(BF16)
        more = mm(left, right, NT)
        found = more if found is None else found + more
    lane_block = iota((L_ROWS, 128), 1) >> 5
    tail = jnp.concatenate([found[:, 128:QUADS]] * 4, axis=1)
    for t in range(W_TILES):
        merged = None
        for c in range(4):
            of_c = (found[:, :128] if t < 4 else tail)[L_ROWS * c : L_ROWS * (c + 1)]
            shift = 32 * (c - t) % 128
            if t < 4 and shift:
                of_c = pltpu.roll(of_c, shift, 1)
            merged = of_c if merged is None else jnp.where(lane_block == c, of_c, merged)
        for i in range(L_ROWS // 8):
            hist[t * (L_ROWS // 8) + i] = merged[8 * i : 8 * i + 8]
    hist_sib_copy().start()

    lanes = lambda part, first, n: table.at[:, pl.ds(part * both + first, n)]
    fill_plane(coords[0:1], coords[1:2], lanes(0, 0, slots), lanes(1, 0, slots))
    z = column(coords[2:3])
    acc[...] = sums_of(z * q, table[:, :slots], table[:, both : both + slots])
    hist_sib_copy().wait_recv()
    hist_chip[...] = hist[...] + hist_sib[...]
    each(ys, lambda o: hist_copy(o).start())

    def take(o, buf):
        fill_plane(got_ion[o, 0:1], got_ion[o, 1:2], buf.at[:, pl.ds(0, slots)], buf.at[:, pl.ds(slots, slots)])

    def add(o, buf):
        v = column(got_ion[o, 2:3], got_ion[o, 3:4])
        acc[...] += sums_of(v, buf[:, :slots], buf[:, slots:])

    if chips <= 16:
        for o in range(1, chips):
            ion_copy(o).wait_recv()
            take(o, (even, odd)[o % 2])
            if o > 1:
                add(o - 1, (even, odd)[(o - 1) % 2])
        add(chips - 1, (even, odd)[(chips - 1) % 2])
    else:

        def one(o):
            ion_copy(o).wait_recv()
            take(o, even)
            add(o, even)

        pl.loop(1, chips)(one)
    for i in range(2 * L_ROWS // 8):
        for t in range(W_TILES):
            sums[i * W_TILES + t] = acc[8 * i : 8 * i + 8, 128 * t : 128 * t + 128]
    sums_copy().start()

    each(devices, lambda o: mail_copy(o).wait_recv())
    got_mail[0] = mail[me]
    arrived = []
    for t in range(devices // per_tile):
        tile = jnp.zeros((4, 128), F32)
        for s in range(t * per_tile, (t + 1) * per_tile):
            db = lax.rem(blk - s // rows + blks, blks)
            dr = lax.rem(row - s % rows + rows, rows)
            tile = tile + got_mail[db * rows + dr]
        arrived.append(tile)
    came = jnp.concatenate(arrived, axis=1)
    came = jnp.concatenate([came, jnp.zeros_like(came)])
    loads[5].wait()
    index = recv_index[...].reshape(1, atoms)
    picks = jnp.where(index == iota((came.shape[1], atoms), 0), 1.0, 0.0).astype(BF16)
    ions = mm3(came, picks, NN)
    fill_plane(ions[0:1], ions[1:2], lanes(0, slots, atoms), lanes(1, slots, atoms))
    z = jnp.concatenate([z, column(ions[2:3])], axis=1)
    charge = jnp.concatenate([q, ions[3:4]], axis=1)

    each(ys, lambda o: hist_copy(o).wait_recv())
    times = hist_chip[...]
    for o in range(1, ys):
        times = times + got_hist[o]
    hf, kf, block, regular = lane_waves()
    l_col = (iota((L_ROWS, 1), 0) + 1).astype(F32)
    px, py, pz = TWO_PI * hf, TWO_PI * kf, TWO_PI * l_col / BOX_Z
    k2 = px * px + py * py + pz * pz
    weight = jnp.exp(-k2 / (4.0 * EWALD_BETA * EWALD_BETA)) / k2
    mix = []
    for t in range(W_TILES):
        at = slice(128 * t, 128 * t + 128)
        n = t * (L_ROWS // 8)
        m = jnp.concatenate([times[n + i] for i in range(L_ROWS // 8)]) * weight[:, at]
        rolled = [m] + [pltpu.roll(m, 32 * i, 1) for i in range(1, 4)]
        b = block[:, at]

        def spread(c):
            value = rolled[(3 - c) % 4]
            for n in range(3):
                value = jnp.where(b == n, rolled[(n - c) % 4], value)
            return value

        m0, m1, m2, m3 = (spread(c) for c in range(4))
        if 32 * (t + 1) > REGULAR:
            reg, is_odd = regular[:, at], (b & 1) == 1
            m0, m2 = (
                jnp.where(reg, m0, jnp.where(is_odd, m1, m0)),
                jnp.where(reg, m2, jnp.where(is_odd, m3, m2)),
            )
            m1, m3 = jnp.where(reg, m1, 0.0), jnp.where(reg, m3, 0.0)
        m1 = jnp.where(b < 2, -m1, m1)
        m2 = jnp.where((b == 0) | (b == 3), -m2, m2)
        m3 = jnp.where((b & 1) == 0, -m3, m3)
        mix.append((m0, m1, m2, m3))

    sums_copy().wait_recv()
    c_x, c_y = [], []
    c_all = []
    for t in range(W_TILES):
        at = slice(128 * t, 128 * t + 128)
        b = block[:, at]
        even_b = (b & 1) == 0
        total = jnp.concatenate(
            [sums[i * W_TILES + t] + from_sib[i * W_TILES + t] for i in range(2 * L_ROWS // 8)]
        )
        m0, m1, m2, m3 = mix[t]

        def partners(v):
            r1, r2, r3 = (pltpu.roll(v, 32 * i, 1) for i in range(1, 4))
            return jnp.where(even_b, r3, r1), r2, jnp.where(even_b, r1, r3)

        t1, t2, t3 = partners(total)
        re, im = slice(0, L_ROWS), slice(L_ROWS, 2 * L_ROWS)
        c = jnp.concatenate(
            [
                m0 * total[re] + m1 * t1[re] + m2 * t2[im] + m3 * t3[im],
                m0 * total[im] + m1 * t1[im] - m2 * t2[re] - m3 * t3[re],
            ]
        )
        _, c2, c3 = partners(c)
        h, k, reg = hf[:, at], kf[:, at], regular[:, at]
        c_all.append(c)
        c_x.append(c2 * jnp.where((b == 1) | (b == 2), -h, h))
        k_signed = jnp.where(even_b, k, -k)
        if 32 * (t + 1) > REGULAR:
            lone = jnp.where(b == 1, k, jnp.where(b == 3, -k, 0.0))
            c_y.append(c3 * jnp.where(reg, k_signed, 0.0) + c2 * jnp.where(reg, 0.0, lone))
        else:
            c_y.append(c3 * k_signed)
    ch, cl = split2(
        jnp.concatenate([jnp.concatenate(v, axis=1) for v in (c_all, c_x, c_y)])
    )
    n = ch.shape[0]
    x = mm(jnp.concatenate([ch, cl]), table[:, :both], NN)
    x = x[:n] + x[n:] + mm(ch, table[:, both:], NN)
    zc, zs = z[:L_ROWS], z[L_ROWS:]
    fz = jnp.sum(
        (x[L_ROWS : 2 * L_ROWS] * zc - x[:L_ROWS] * zs) * l_col, axis=0, keepdims=True
    )
    fx = jnp.sum(x[2 * L_ROWS : 4 * L_ROWS] * z, axis=0, keepdims=True)
    fy = jnp.sum(x[4 * L_ROWS :] * z, axis=0, keepdims=True)
    gain = (-scale * TWO_PI) * charge
    forces[...] = gain * jnp.concatenate([fx, fy, fz * (1.0 / BOX_Z)])

    each(chips, lambda o: ion_copy(o).wait_send())
    each(devices, lambda o: mail_copy(o).wait_send())
    hist_sib_copy().wait_send()
    each(ys, lambda o: hist_copy(o).wait_send())
    sums_copy().wait_send()


def deliver(counts, forces, slot_forces, atom_forces):
    slots = slot_forces.shape[1]
    live = iota((1, slots), 1) < jnp.broadcast_to(counts[...].reshape(1, 1), (1, slots))
    slot_forces[...] = jnp.where(live, forces[:, :slots], 0.0)
    atom_forces[...] = forces[:, slots:]


VMEM = pl.BlockSpec(memory_space=pltpu.VMEM)
ANY = pl.BlockSpec(memory_space=pl.ANY)


def body(coords, charges, counts, send_slot, recv_index, wave_ints):
    slots = charges.shape[0]
    atoms = recv_index.shape[0]
    blks, rows = lax.axis_size("blk"), lax.axis_size("row")
    devices = blks * rows
    chips = devices // 2
    cap = 2 * atoms // devices
    scale = FORCE_GAIN / math.sqrt(float(atoms * devices * blks * wave_ints.shape[1]))
    shape = jax.ShapeDtypeStruct
    args = (coords, charges, counts, send_slot, recv_index, wave_ints)
    dma = lambda n: [pltpu.SemaphoreType.DMA((n,))] * 2
    forces = pl.pallas_call(
        functools.partial(kernel, blks, rows, cap, scale),
        out_shape=shape((3, slots + atoms), F32),
        in_specs=[ANY] * 6,
        out_specs=VMEM,
        scratch_shapes=[pltpu.VMEM(a.shape, a.dtype) for a in args]
        + [
            pltpu.VMEM((WAVES, 2 * (slots + atoms)), BF16),
            pltpu.VMEM((WAVES, 2 * slots), BF16),
            pltpu.VMEM((WAVES, 2 * slots), BF16),
            pltpu.VMEM((4, slots), F32),
            pltpu.VMEM((chips, 4, slots), F32),
            pltpu.VMEM((devices, 4, 128), F32),
            pltpu.VMEM((devices, 4, 128), F32),
            pltpu.VMEM((H_TILES, 8, 128), F32),
            pltpu.VMEM((H_TILES, 8, 128), F32),
            pltpu.VMEM((H_TILES, 8, 128), F32),
            pltpu.VMEM((blks // 2, H_TILES, 8, 128), F32),
            pltpu.VMEM((2 * L_ROWS, WAVES), F32),
            pltpu.VMEM((T_TILES, 8, 128), F32),
            pltpu.VMEM((T_TILES, 8, 128), F32),
        ]
        + [pltpu.SemaphoreType.DMA((6,))]
        + dma(chips) + dma(devices) + dma(1) + dma(blks // 2) + dma(1),
        compiler_params=pltpu.CompilerParams(
            collective_id=0, has_side_effects=True, vmem_limit_bytes=56 * 2**20
        ),
    )(*args)
    return pl.pallas_call(
        deliver,
        out_shape=[shape((3, slots), F32), shape((3, atoms), F32)],
        in_specs=[VMEM] * 2,
        out_specs=[VMEM] * 2,
    )(counts, forces)


def solution(mesh):
    ions = P(("groups", "blk", "row"))
    return jax.shard_map(
        body,
        mesh=mesh,
        in_specs=(P(None, *ions), ions, ions, ions, ions, P(None, "blk")),
        out_specs=(P(None, *ions), P(None, *ions)),
        check_vma=False,
    )
```

time: 27.4 us -> 27.7 us (1.011)
  the two profiles are of different devices: /device:TPU:1 before, /device:TPU:0 now
where the time goes in v1:
time: 27.7 us; the launch traced here: 27.5 us
  Pallas kernels  26.2 us (95%)
  between operations  1.28 us (5%)
    pallas_call x1, Pallas kernels, body(): pl.pallas_call(functools.partial(kernel, blks, rows, cap, scale), out_sha...  24.8 us
    pallas_call x1, Pallas kernels, body(): pl.pallas_call(deliver, out_shape=[shape((3, slots), F32), shape((3, atom...  1.4 us

profile of v1, /device:TPU:0, one launch (start us, length us, event | category | flops | bytes accessed | tf_op | source)
XLA Modules:
  0.0 27.5 jit_solution(2665718040564030583)
XLA Ops:
  1.3 24.8 %shard_map.77.forces = f32[3,1280]{1,0:T(4,128)} custom-call(f32[3,768]{1,0:T(4,128)} %coords_in.1, f32[768]{0:T(1024)} %charges_in.1, s32[1]{0:T(128)S(6)} %copy.8.counts_in.counts, s32[768]{0:T(1024)} %send_in.1, s32[512]{0:T(512)} %recv_in.1, s32[3,6144]{1,0:T(4,128)} %wave_in.1), custom_call_target="tpu_custom_call" | custom-call | tf_op jit(solution)/shard_map/pallas_call | solution.py:475
  26.1 1.4 %shard_map.78 = (f32[3,768]{1,0:T(4,128)}, f32[3,512]{1,0:T(4,128)}) custom-call(s32[1]{0:T(128)S(6)} %copy.8.counts_in.counts, f32[3,1280]{1,0:T(4,128)} %shard_map.77.forces), custom_call_target="tpu_custom_call" | custom-call | tf_op jit(solution)/shard_map/pallas_call | solution.py:503

commit v2 on v1

--- a/solution.py
+++ b/solution.py
@@ -151,9 +151,8 @@
 
 
 def sums_of(v, hi, lo):
-    vh, vl = split2(v)
-    out = mm(jnp.concatenate([vh, vl]), hi, NT)
-    return out[: 2 * L_ROWS] + out[2 * L_ROWS :] + mm(vh, lo, NT)
+    out = mm(v[...], hi, NT)
+    return out[: 2 * L_ROWS] + out[2 * L_ROWS :] + mm(v[: 2 * L_ROWS], lo, NT)
 
 
 def each(count, f):
@@ -170,7 +169,7 @@
     forces,
     coords, charges, counts, send_slot, recv_index, wave,
     table, even, odd, ion, got_ion, mail, got_mail,
-    hist, hist_sib, hist_chip, got_hist, acc, sums, from_sib,
+    hist, hist_sib, hist_chip, got_hist, acc, sums, from_sib, coefs, zed, gain, found, even_v, odd_v,
     in_s, i_s, i_r, m_s, m_r, h_s, h_r, y_s, y_r, x_s, x_r,
 ):
     devices = blks * rows
@@ -267,9 +266,10 @@
     loads[4].wait()
     k_local = wave.shape[1]
     part = 1536 if k_local % 1536 == 0 else k_local
-    found = None
-    for first in range(0, k_local, part):
-        w = wave[:, first : first + part]
+    found[...] = jnp.zeros_like(found)
+
+    def count(i):
+        w = wave[:, pl.ds(pl.multiple_of(i * part, 128), part)]
         h, k, l = w[0:1], w[1:2], w[2:3]
         flip = l < 0
         s1 = jnp.where((h < 0) ^ flip, -1.0, 1.0)
@@ -287,8 +287,10 @@
         of_l = l == iota((L_ROWS, part), 0) + 1
         left = jnp.concatenate([jnp.where(of_l, s, 0.0).astype(BF16) for s in signs])
         right = jnp.where(quad_of(h, k) == iota((QUADS, part), 0), 1.0, 0.0).astype(BF16)
-        more = mm(left, right, NT)
-        found = more if found is None else found + more
+        half = part // 2
+        found[...] += mm(left[:, :half], right[:, :half], NT) + mm(left[:, half:], right[:, half:], NT)
+
+    pl.loop(0, k_local // part)(count)
     lane_block = iota((L_ROWS, 128), 1) >> 5
     tail = jnp.concatenate([found[:, 128:QUADS]] * 4, axis=1)
     for t in range(W_TILES):
@@ -306,33 +308,36 @@
     lanes = lambda part, first, n: table.at[:, pl.ds(part * both + first, n)]
     fill_plane(coords[0:1], coords[1:2], lanes(0, 0, slots), lanes(1, 0, slots))
     z = column(coords[2:3])
-    acc[...] = sums_of(z * q, table[:, :slots], table[:, both : both + slots])
+
+    def put(v, value):
+        v[: 2 * L_ROWS], v[2 * L_ROWS :] = split2(value)
+
+    def take(o, buf, v):
+        put(v, column(got_ion[o, 2:3], got_ion[o, 3:4]))
+        fill_plane(got_ion[o, 0:1], got_ion[o, 1:2], buf.at[:, pl.ds(0, slots)], buf.at[:, pl.ds(slots, slots)])
+
+    def add(buf, v):
+        acc[...] += sums_of(v, buf[:, :slots], buf[:, slots:])
+
+    put(even_v, z * q)
     hist_sib_copy().wait_recv()
     hist_chip[...] = hist[...] + hist_sib[...]
     each(ys, lambda o: hist_copy(o).start())
-
-    def take(o, buf):
-        fill_plane(got_ion[o, 0:1], got_ion[o, 1:2], buf.at[:, pl.ds(0, slots)], buf.at[:, pl.ds(slots, slots)])
-
-    def add(o, buf):
-        v = column(got_ion[o, 2:3], got_ion[o, 3:4])
-        acc[...] += sums_of(v, buf[:, :slots], buf[:, slots:])
-
-    if chips <= 16:
-        for o in range(1, chips):
-            ion_copy(o).wait_recv()
-            take(o, (even, odd)[o % 2])
-            if o > 1:
-                add(o - 1, (even, odd)[(o - 1) % 2])
-        add(chips - 1, (even, odd)[(chips - 1) % 2])
-    else:
-
-        def one(o):
-            ion_copy(o).wait_recv()
-            take(o, even)
-            add(o, even)
-
-        pl.loop(1, chips)(one)
+    ion_copy(1).wait_recv()
+    acc[...] = sums_of(even_v, table[:, :slots], table[:, both : both + slots])
+    take(1, odd, odd_v)
+
+    def pair(i):
+        o = 2 * i + 2
+        ion_copy(o).wait_recv()
+        add(odd, odd_v)
+        take(o, even, even_v)
+        ion_copy(o + 1).wait_recv()
+        add(even, even_v)
+        take(o + 1, odd, odd_v)
+
+    pl.loop(0, chips // 2 - 1)(pair)
+    add(odd, odd_v)
     for i in range(2 * L_ROWS // 8):
         for t in range(W_TILES):
             sums[i * W_TILES + t] = acc[8 * i : 8 * i + 8, 128 * t : 128 * t + 128]
@@ -355,8 +360,9 @@
     picks = jnp.where(index == iota((came.shape[1], atoms), 0), 1.0, 0.0).astype(BF16)
     ions = mm3(came, picks, NN)
     fill_plane(ions[0:1], ions[1:2], lanes(0, slots, atoms), lanes(1, slots, atoms))
-    z = jnp.concatenate([z, column(ions[2:3])], axis=1)
-    charge = jnp.concatenate([q, ions[3:4]], axis=1)
+    zed[:, :slots] = z
+    zed[:, slots:] = column(ions[2:3])
+    gain[...] = (-scale * TWO_PI) * jnp.concatenate([q, ions[3:4]], axis=1)
 
     each(ys, lambda o: hist_copy(o).wait_recv())
     times = hist_chip[...]
@@ -432,16 +438,24 @@
         jnp.concatenate([jnp.concatenate(v, axis=1) for v in (c_all, c_x, c_y)])
     )
     n = ch.shape[0]
-    x = mm(jnp.concatenate([ch, cl]), table[:, :both], NN)
-    x = x[:n] + x[n:] + mm(ch, table[:, both:], NN)
-    zc, zs = z[:L_ROWS], z[L_ROWS:]
-    fz = jnp.sum(
-        (x[L_ROWS : 2 * L_ROWS] * zc - x[:L_ROWS] * zs) * l_col, axis=0, keepdims=True
-    )
-    fx = jnp.sum(x[2 * L_ROWS : 4 * L_ROWS] * z, axis=0, keepdims=True)
-    fy = jnp.sum(x[4 * L_ROWS :] * z, axis=0, keepdims=True)
-    gain = (-scale * TWO_PI) * charge
-    forces[...] = gain * jnp.concatenate([fx, fy, fz * (1.0 / BOX_Z)])
+    coefs[:n] = ch
+    coefs[n:] = cl
+    half = both // 2
+
+    def pull(i):
+        at = pl.ds(pl.multiple_of(i * half, 128), half)
+        x = mm(coefs[...], table[:, at], NN)
+        x = x[:n] + x[n:] + mm(coefs[:n], table[:, pl.ds(pl.multiple_of(both + i * half, 128), half)], NN)
+        zc, zs = zed[:L_ROWS, at], zed[L_ROWS:, at]
+        z = zed[:, at]
+        fz = jnp.sum(
+            (x[L_ROWS : 2 * L_ROWS] * zc - x[:L_ROWS] * zs) * l_col, axis=0, keepdims=True
+        )
+        fx = jnp.sum(x[2 * L_ROWS : 4 * L_ROWS] * z, axis=0, keepdims=True)
+        fy = jnp.sum(x[4 * L_ROWS :] * z, axis=0, keepdims=True)
+        forces[:, at] = gain[:, at] * jnp.concatenate([fx, fy, fz * (1.0 / BOX_Z)])
+
+    pl.loop(0, 2)(pull)
 
     each(chips, lambda o: ion_copy(o).wait_send())
     each(devices, lambda o: mail_copy(o).wait_send())
@@ -493,6 +507,12 @@
             pltpu.VMEM((2 * L_ROWS, WAVES), F32),
             pltpu.VMEM((T_TILES, 8, 128), F32),
             pltpu.VMEM((T_TILES, 8, 128), F32),
+            pltpu.VMEM((12 * L_ROWS, WAVES), BF16),
+            pltpu.VMEM((2 * L_ROWS, slots + atoms), F32),
+            pltpu.VMEM((1, slots + atoms), F32),
+            pltpu.VMEM((4 * L_ROWS, QUADS), F32),
+            pltpu.VMEM((4 * L_ROWS, slots), BF16),
+            pltpu.VMEM((4 * L_ROWS, slots), BF16),
         ]
         + [pltpu.SemaphoreType.DMA((6,))]
         + dma(chips) + dma(devices) + dma(1) + dma(blks // 2) + dma(1),

time: 27.7 us -> 24.9 us (0.90)
  Pallas kernels: 26.2 us -> 23.4 us
    pallas_call x1, Pallas kernels: 24.8 us -> 22 us  [body(): pl.pallas_call(functools.partial(kernel, blks, rows, cap, scale), out_sha...]
where the time goes in v2:
time: 24.9 us; the launch traced here: 24.7 us
  Pallas kernels  23.4 us (94%)
  between operations  1.28 us (5%)
    pallas_call x1, Pallas kernels, body(): pl.pallas_call(functools.partial(kernel, blks, rows, cap, scale), out_sha...  22 us
    pallas_call x1, Pallas kernels, body(): pl.pallas_call(deliver, out_shape=[shape((3, slots), F32), shape((3, atom...  1.4 us

profile of v2, /device:TPU:0, one launch (start us, length us, event | category | flops | bytes accessed | tf_op | source)
XLA Modules:
  0.0 24.7 jit_solution(631804232510816518)
XLA Ops:
  1.3 22.0 %shard_map.77.forces = f32[3,1280]{1,0:T(4,128)} custom-call(f32[3,768]{1,0:T(4,128)} %coords_in.1, f32[768]{0:T(1024)} %charges_in.1, s32[1]{0:T(128)S(6)} %copy.8.counts_in.counts, s32[768]{0:T(1024)} %send_in.1, s32[512]{0:T(512)} %recv_in.1, s32[3,6144]{1,0:T(4,128)} %wave_in.1), custom_call_target="tpu_custom_call" | custom-call | tf_op jit(solution)/shard_map/pallas_call | solution.py:489
  23.3 1.4 %shard_map.78 = (f32[3,768]{1,0:T(4,128)}, f32[3,512]{1,0:T(4,128)}) custom-call(s32[1]{0:T(128)S(6)} %copy.8.counts_in.counts, f32[3,1280]{1,0:T(4,128)} %shard_map.77.forces), custom_call_target="tpu_custom_call" | custom-call | tf_op jit(solution)/shard_map/pallas_call | solution.py:523

commit v3 on v2

--- a/solution.py
+++ b/solution.py
@@ -169,7 +169,7 @@
     forces,
     coords, charges, counts, send_slot, recv_index, wave,
     table, even, odd, ion, got_ion, mail, got_mail,
-    hist, hist_sib, hist_chip, got_hist, acc, sums, from_sib, coefs, zed, gain, found, even_v, odd_v,
+    hist, hist_sib, hist_chip, got_hist, acc, sums, from_sib, zed, gain, found, even_v, odd_v,
     in_s, i_s, i_r, m_s, m_r, h_s, h_r, y_s, y_r, x_s, x_r,
 ):
     devices = blks * rows
@@ -305,7 +305,7 @@
             hist[t * (L_ROWS // 8) + i] = merged[8 * i : 8 * i + 8]
     hist_sib_copy().start()
 
-    lanes = lambda part, first, n: table.at[:, pl.ds(part * both + first, n)]
+    lanes = lambda part, first, n: table.at[pl.ds(part * WAVES, WAVES), pl.ds(first, n)]
     fill_plane(coords[0:1], coords[1:2], lanes(0, 0, slots), lanes(1, 0, slots))
     z = column(coords[2:3])
 
@@ -320,12 +320,13 @@
         acc[...] += sums_of(v, buf[:, :slots], buf[:, slots:])
 
     put(even_v, z * q)
+    ion_copy(1).wait_recv()
+    acc[...] = sums_of(even_v, table[:WAVES, :slots], table[WAVES:, :slots])
+    take(1, odd, odd_v)
+
     hist_sib_copy().wait_recv()
     hist_chip[...] = hist[...] + hist_sib[...]
     each(ys, lambda o: hist_copy(o).start())
-    ion_copy(1).wait_recv()
-    acc[...] = sums_of(even_v, table[:, :slots], table[:, both : both + slots])
-    take(1, odd, odd_v)
 
     def pair(i):
         o = 2 * i + 2
@@ -437,25 +438,16 @@
     ch, cl = split2(
         jnp.concatenate([jnp.concatenate(v, axis=1) for v in (c_all, c_x, c_y)])
     )
-    n = ch.shape[0]
-    coefs[:n] = ch
-    coefs[n:] = cl
-    half = both // 2
-
-    def pull(i):
-        at = pl.ds(pl.multiple_of(i * half, 128), half)
-        x = mm(coefs[...], table[:, at], NN)
-        x = x[:n] + x[n:] + mm(coefs[:n], table[:, pl.ds(pl.multiple_of(both + i * half, 128), half)], NN)
-        zc, zs = zed[:L_ROWS, at], zed[L_ROWS:, at]
-        z = zed[:, at]
-        fz = jnp.sum(
-            (x[L_ROWS : 2 * L_ROWS] * zc - x[:L_ROWS] * zs) * l_col, axis=0, keepdims=True
-        )
-        fx = jnp.sum(x[2 * L_ROWS : 4 * L_ROWS] * z, axis=0, keepdims=True)
-        fy = jnp.sum(x[4 * L_ROWS :] * z, axis=0, keepdims=True)
-        forces[:, at] = gain[:, at] * jnp.concatenate([fx, fy, fz * (1.0 / BOX_Z)])
-
-    pl.loop(0, 2)(pull)
+    x = mm(jnp.concatenate([ch, ch], axis=1), table[...], NN)
+    x = x + mm(cl, table[:WAVES], NN)
+    z = zed[...]
+    zc, zs = z[:L_ROWS], z[L_ROWS:]
+    fz = jnp.sum(
+        (x[L_ROWS : 2 * L_ROWS] * zc - x[:L_ROWS] * zs) * l_col, axis=0, keepdims=True
+    )
+    fx = jnp.sum(x[2 * L_ROWS : 4 * L_ROWS] * z, axis=0, keepdims=True)
+    fy = jnp.sum(x[4 * L_ROWS :] * z, axis=0, keepdims=True)
+    forces[...] = gain[...] * jnp.concatenate([fx, fy, fz * (1.0 / BOX_Z)])
 
     each(chips, lambda o: ion_copy(o).wait_send())
     each(devices, lambda o: mail_copy(o).wait_send())
@@ -493,7 +485,7 @@
         out_specs=VMEM,
         scratch_shapes=[pltpu.VMEM(a.shape, a.dtype) for a in args]
         + [
-            pltpu.VMEM((WAVES, 2 * (slots + atoms)), BF16),
+            pltpu.VMEM((2 * WAVES, slots + atoms), BF16),
             pltpu.VMEM((WAVES, 2 * slots), BF16),
             pltpu.VMEM((WAVES, 2 * slots), BF16),
             pltpu.VMEM((4, slots), F32),
@@ -507,7 +499,6 @@
             pltpu.VMEM((2 * L_ROWS, WAVES), F32),
             pltpu.VMEM((T_TILES, 8, 128), F32),
             pltpu.VMEM((T_TILES, 8, 128), F32),
-            pltpu.VMEM((12 * L_ROWS, WAVES), BF16),
             pltpu.VMEM((2 * L_ROWS, slots + atoms), F32),
             pltpu.VMEM((1, slots + atoms), F32),
             pltpu.VMEM((4 * L_ROWS, QUADS), F32),

time: 24.9 us -> 23.7 us (0.952)
  Pallas kernels: 23.4 us -> 22.2 us
    pallas_call x1, Pallas kernels: 22 us -> 20.8 us  [body(): pl.pallas_call(functools.partial(kernel, blks, rows, cap, scale), out_sha...]
where the time goes in v3:
time: 23.7 us; the launch traced here: 23.4 us
  Pallas kernels  22.2 us (94%)
  between operations  1.28 us (5%)
    pallas_call x1, Pallas kernels, body(): pl.pallas_call(functools.partial(kernel, blks, rows, cap, scale), out_sha...  20.8 us
    pallas_call x1, Pallas kernels, body(): pl.pallas_call(deliver, out_shape=[shape((3, slots), F32), shape((3, atom...  1.4 us

profile of v3, /device:TPU:0, one launch (start us, length us, event | category | flops | bytes accessed | tf_op | source)
XLA Modules:
  0.0 23.4 jit_solution(1318786595109636945)
XLA Ops:
  1.3 20.8 %shard_map.77.forces = f32[3,1280]{1,0:T(4,128)} custom-call(f32[3,768]{1,0:T(4,128)} %coords_in.1, f32[768]{0:T(1024)} %charges_in.1, s32[1]{0:T(128)S(6)} %copy.8.counts_in.counts, s32[768]{0:T(1024)} %send_in.1, s32[512]{0:T(512)} %recv_in.1, s32[3,6144]{1,0:T(4,128)} %wave_in.1), custom_call_target="tpu_custom_call" | custom-call | tf_op jit(solution)/shard_map/pallas_call | solution.py:481
  22.0 1.4 %shard_map.78 = (f32[3,768]{1,0:T(4,128)}, f32[3,512]{1,0:T(4,128)}) custom-call(s32[1]{0:T(128)S(6)} %copy.8.counts_in.counts, f32[3,1280]{1,0:T(4,128)} %shard_map.77.forces), custom_call_target="tpu_custom_call" | custom-call | tf_op jit(solution)/shard_map/pallas_call | solution.py:514

commit v4 on v3

--- a/solution.py
+++ b/solution.py
@@ -166,7 +166,7 @@
 def kernel(
     blks, rows, cap, scale,
     coords_in, charges_in, counts_in, send_in, recv_in, wave_in,
-    forces,
+    slot_forces, atom_forces,
     coords, charges, counts, send_slot, recv_index, wave,
     table, even, odd, ion, got_ion, mail, got_mail,
     hist, hist_sib, hist_chip, got_hist, acc, sums, from_sib, zed, gain, found, even_v, odd_v,
@@ -207,8 +207,8 @@
 
     def other_chip(o):
         if isinstance(o, int):
-            return {"blk": blk_at[2 * (o // rows)], "row": row_at[o % rows]}
-        return other(2 * rows * lax.div(o, rows) + lax.rem(o, rows))
+            return {"blk": blk_at[2 * (o % ys)], "row": row_at[o // ys]}
+        return {"blk": lax.rem(blk + 2 * lax.rem(o, ys), blks), "row": lax.rem(row + lax.div(o, ys), rows)}
 
     def copy(src, dst, s, r, o, dev):
         return pltpu.make_async_remote_copy(
@@ -227,7 +227,7 @@
         return copy(hist, hist_sib, h_s, h_r, 0, sibling)
 
     def hist_copy(o):
-        return copy(hist_chip, got_hist.at[o], y_s, y_r, o, other_chip(o * rows))
+        return copy(hist_chip, got_hist.at[o], y_s, y_r, o, other_chip(o))
 
     def sums_copy():
         return copy(sums, from_sib, x_s, x_r, 0, sibling)
@@ -250,17 +250,23 @@
     each(chips, lambda o: ion_copy(o).start())
 
     loads[3].wait()
-    target = jnp.where(live, send_slot[...].reshape(1, slots), -1)
-    spots = jnp.where(target == iota((devices * cap, slots), 0), 1.0, 0.0).astype(BF16)
-    entries = jnp.concatenate([coords[...], q, jnp.zeros((4, slots), F32)])
-    out = mm3(entries, spots, NT)
     per_tile = 128 // cap
-    lane_part = iota((8, 128), 1) // cap
+    target = jnp.where(live, send_slot[...].reshape(1, slots), -cap)
+    dest = lax.shift_right_arithmetic(target, cap.bit_length() - 1)
+    lane = (target & (cap - 1)) + lax.rem(me, per_tile) * cap
+    spots = jnp.where(lane == iota((128, slots), 0), 1.0, 0.0).astype(BF16)
+    quad = jnp.concatenate([coords[...], q] * 2)
+    terms = [term.astype(F32) for term in split3(quad)]
+    half = lax.shift_right_logical(iota((8, slots), 0), 2)
+    places = [dest == half + d for d in range(0, devices, 2)]
+    rows_of = [
+        jnp.where(at, term, 0.0).astype(BF16) for term in terms for at in places
+    ]
+    out = mm(jnp.concatenate(rows_of), spots, NT)
+    n = 4 * devices
+    out = out[:n] + out[n : 2 * n] + out[2 * n :]
     for d in range(devices):
-        tile = out[:, 128 * (d // per_tile) : 128 * (d // per_tile) + 128]
-        tile = jnp.where(lane_part == d % per_tile, tile, 0.0)
-        shift = (me % per_tile - d % per_tile + per_tile) % per_tile * cap
-        mail[d] = pltpu.roll(tile, shift, 1)[:4]
+        mail[d] = out[4 * d : 4 * d + 4]
     each(devices, lambda o: mail_copy(o).start())
 
     loads[4].wait()
@@ -331,9 +337,9 @@
     def pair(i):
         o = 2 * i + 2
         ion_copy(o).wait_recv()
+        ion_copy(o + 1).wait_recv()
         add(odd, odd_v)
         take(o, even, even_v)
-        ion_copy(o + 1).wait_recv()
         add(even, even_v)
         take(o + 1, odd, odd_v)
 
@@ -347,19 +353,21 @@
     each(devices, lambda o: mail_copy(o).wait_recv())
     got_mail[0] = mail[me]
     arrived = []
-    for t in range(devices // per_tile):
-        tile = jnp.zeros((4, 128), F32)
-        for s in range(t * per_tile, (t + 1) * per_tile):
-            db = lax.rem(blk - s // rows + blks, blks)
-            dr = lax.rem(row - s % rows + rows, rows)
-            tile = tile + got_mail[db * rows + dr]
-        arrived.append(tile)
-    came = jnp.concatenate(arrived, axis=1)
-    came = jnp.concatenate([came, jnp.zeros_like(came)])
+    for s in range(devices):
+        db = lax.rem(blk - s // rows + blks, blks)
+        dr = lax.rem(row - s % rows + rows, rows)
+        arrived.append(got_mail[db * rows + dr])
     loads[5].wait()
     index = recv_index[...].reshape(1, atoms)
-    picks = jnp.where(index == iota((came.shape[1], atoms), 0), 1.0, 0.0).astype(BF16)
-    ions = mm3(came, picks, NN)
+    rank = index & (cap - 1)
+    source = lax.shift_right_logical(index, cap.bit_length() - 1)
+    picks = jnp.where(rank == (iota((128, atoms), 0) & (cap - 1)), 1.0, 0.0).astype(BF16)
+    came = mm3(jnp.concatenate(arrived), picks, NN)
+    half = lax.shift_right_logical(iota((8, atoms), 0), 2)
+    ions = jnp.zeros((8, atoms), F32)
+    for s in range(0, devices, 2):
+        ions = ions + jnp.where(source == half + s, came[4 * s : 4 * s + 8], 0.0)
+    ions = ions[:4] + ions[4:]
     fill_plane(ions[0:1], ions[1:2], lanes(0, slots, atoms), lanes(1, slots, atoms))
     zed[:, :slots] = z
     zed[:, slots:] = column(ions[2:3])
@@ -447,7 +455,9 @@
     )
     fx = jnp.sum(x[2 * L_ROWS : 4 * L_ROWS] * z, axis=0, keepdims=True)
     fy = jnp.sum(x[4 * L_ROWS :] * z, axis=0, keepdims=True)
-    forces[...] = gain[...] * jnp.concatenate([fx, fy, fz * (1.0 / BOX_Z)])
+    force = gain[...] * jnp.concatenate([fx, fy, fz * (1.0 / BOX_Z)])
+    slot_forces[...] = jnp.where(live, force[:, :slots], 0.0)
+    atom_forces[...] = force[:, slots:]
 
     each(chips, lambda o: ion_copy(o).wait_send())
     each(devices, lambda o: mail_copy(o).wait_send())
@@ -456,14 +466,19 @@
     sums_copy().wait_send()
 
 
-def deliver(counts, forces, slot_forces, atom_forces):
-    slots = slot_forces.shape[1]
-    live = iota((1, slots), 1) < jnp.broadcast_to(counts[...].reshape(1, 1), (1, slots))
-    slot_forces[...] = jnp.where(live, forces[:, :slots], 0.0)
-    atom_forces[...] = forces[:, slots:]
+def deliver(slot_in, atom_in, slot_forces, atom_forces, sem):
+    copies = [
+        pltpu.make_async_copy(slot_in, slot_forces, sem.at[0]),
+        pltpu.make_async_copy(atom_in, atom_forces, sem.at[1]),
+    ]
+    for copy in copies:
+        copy.start()
+    for copy in copies:
+        copy.wait()
 
 
 VMEM = pl.BlockSpec(memory_space=pltpu.VMEM)
+HBM = pl.BlockSpec(memory_space=pltpu.HBM)
 ANY = pl.BlockSpec(memory_space=pl.ANY)
 
 
@@ -478,11 +493,11 @@
     shape = jax.ShapeDtypeStruct
     args = (coords, charges, counts, send_slot, recv_index, wave_ints)
     dma = lambda n: [pltpu.SemaphoreType.DMA((n,))] * 2
-    forces = pl.pallas_call(
+    slot_forces, atom_forces = pl.pallas_call(
         functools.partial(kernel, blks, rows, cap, scale),
-        out_shape=shape((3, slots + atoms), F32),
-        in_specs=[ANY] * 6,
-        out_specs=VMEM,
+        out_shape=[pltpu.VMEM((3, slots), F32), pltpu.VMEM((3, atoms), F32)],
+        in_specs=[HBM] * 6,
+        out_specs=[VMEM] * 2,
         scratch_shapes=[pltpu.VMEM(a.shape, a.dtype) for a in args]
         + [
             pltpu.VMEM((2 * WAVES, slots + atoms), BF16),
@@ -511,12 +526,7 @@
             collective_id=0, has_side_effects=True, vmem_limit_bytes=56 * 2**20
         ),
     )(*args)
-    return pl.pallas_call(
-        deliver,
-        out_shape=[shape((3, slots), F32), shape((3, atoms), F32)],
-        in_specs=[VMEM] * 2,
-        out_specs=[VMEM] * 2,
-    )(counts, forces)
+    return slot_forces, atom_forces
 
 
 def solution(mesh):

time: 23.7 us -> 21.2 us (0.89)
  Pallas kernels: 22.2 us -> 18.5 us
  local copies, waits for them, and re-layouts: 0 us -> 1.2 us
    pallas_call x1, Pallas kernels: 20.8 us -> 18.5 us  [body(): pl.pallas_call(functools.partial(kernel, blks, rows, cap, scale), out_sha...]
    pallas_call x1 -> x0, Pallas kernels: 1.4 us -> none  [body(): pl.pallas_call(deliver, out_shape=[shape((3, slots), F32), shape((3, atom...]
    unnamed x0 -> x2, local copies, waits for them, and re-layouts: none -> 1.2 us
where the time goes in v4:
time: 21.2 us; the launch traced here: 21 us
  Pallas kernels  18.5 us (87%)
  between operations  1.28 us (6%)
  local copies, waits for them, and re-layouts  1.2 us (6%)
    pallas_call x1, Pallas kernels, body(): pl.pallas_call(functools.partial(kernel, blks, rows, cap, scale), out_sha...  18.5 us
    unnamed x2, local copies, waits for them, and re-layouts  1.2 us

profile of v4, /device:TPU:0, one launch (start us, length us, event | category | flops | bytes accessed | tf_op | source)
XLA Modules:
  0.0 21.0 jit_solution(14257993640609585789)
XLA Ops:
  1.3 18.5 %shard_map.77 = (f32[3,768]{1,0:T(4,128)S(1)}, f32[3,512]{1,0:T(4,128)S(1)}) custom-call(f32[3,768]{1,0:T(4,128)} %coords_in.1, f32[768]{0:T(1024)} %charges_in.1, s32[1]{0:T(128)S(6)} %copy.12.counts_in, s32[768]{0:T(1024)} %send_in.1, s32[512]{0:T(512)} %recv_in.1, s32[3,6144]{1,0:T(4,128)} %wave_in.1), custom_call_target="tpu_custom_call" | custom-call | tf_op jit(solution)/shard_map/pallas_call | solution.py:496
  19.8 0.6 %copy.10 = f32[3,768]{1,0:T(4,128)} copy(f32[3,768]{1,0:T(4,128)S(1)} %get-tuple-element.2) | data formatting | bytes 18432
  20.4 0.6 %copy.11 = f32[3,512]{1,0:T(4,128)} copy(f32[3,512]{1,0:T(4,128)S(1)} %get-tuple-element.3) | data formatting | bytes 12288

commit v5 on v4

--- a/solution.py
+++ b/solution.py
@@ -343,8 +343,22 @@
         add(even, even_v)
         take(o + 1, odd, odd_v)
 
-    pl.loop(0, chips // 2 - 1)(pair)
-    add(odd, odd_v)
+    if chips <= 8:
+
+        def rest(_):
+            for o in range(2, chips):
+                ion_copy(o).wait_recv()
+            for o in range(2, chips, 2):
+                add(odd, odd_v)
+                take(o, even, even_v)
+                add(even, even_v)
+                take(o + 1, odd, odd_v)
+            add(odd, odd_v)
+
+        pl.loop(0, 1 + lax.div(blk, blks))(rest)
+    else:
+        pl.loop(0, chips // 2 - 1)(pair)
+        add(odd, odd_v)
     for i in range(2 * L_ROWS // 8):
         for t in range(W_TILES):
             sums[i * W_TILES + t] = acc[8 * i : 8 * i + 8, 128 * t : 128 * t + 128]

time: 21.2 us -> 20.5 us (0.967)
  Pallas kernels: 18.5 us -> 17.8 us
    pallas_call x1, Pallas kernels: 18.5 us -> 17.8 us  [body(): pl.pallas_call(functools.partial(kernel, blks, rows, cap, scale), out_sha...]
where the time goes in v5:
time: 20.5 us; the launch traced here: 20.3 us
  Pallas kernels  17.8 us (87%)
  between operations  1.28 us (6%)
  local copies, waits for them, and re-layouts  1.2 us (6%)
    pallas_call x1, Pallas kernels, body(): pl.pallas_call(functools.partial(kernel, blks, rows, cap, scale), out_sha...  17.8 us
    unnamed x2, local copies, waits for them, and re-layouts  1.2 us

profile of v5, /device:TPU:0, one launch (start us, length us, event | category | flops | bytes accessed | tf_op | source)
XLA Modules:
  0.0 20.3 jit_solution(8169346655120714365)
XLA Ops:
  1.3 17.8 %shard_map.77 = (f32[3,768]{1,0:T(4,128)S(1)}, f32[3,512]{1,0:T(4,128)S(1)}) custom-call(f32[3,768]{1,0:T(4,128)} %coords_in.1, f32[768]{0:T(1024)} %charges_in.1, s32[1]{0:T(128)S(6)} %copy.12.counts_in, s32[768]{0:T(1024)} %send_in.1, s32[512]{0:T(512)} %recv_in.1, s32[3,6144]{1,0:T(4,128)} %wave_in.1), custom_call_target="tpu_custom_call" | custom-call | tf_op jit(solution)/shard_map/pallas_call | solution.py:510
  19.1 0.6 %copy.10 = f32[3,768]{1,0:T(4,128)} copy(f32[3,768]{1,0:T(4,128)S(1)} %get-tuple-element.2) | data formatting | bytes 18432
  19.7 0.6 %copy.11 = f32[3,512]{1,0:T(4,128)} copy(f32[3,512]{1,0:T(4,128)S(1)} %get-tuple-element.3) | data formatting | bytes 12288

commit v6 on v5

--- a/solution.py
+++ b/solution.py
@@ -148,11 +148,6 @@
         cs.append(c)
         ss.append(s)
     return jnp.concatenate(cs + ss)
-
-
-def sums_of(v, hi, lo):
-    out = mm(v[...], hi, NT)
-    return out[: 2 * L_ROWS] + out[2 * L_ROWS :] + mm(v[: 2 * L_ROWS], lo, NT)
 
 
 def each(count, f):
@@ -322,12 +317,14 @@
         put(v, column(got_ion[o, 2:3], got_ion[o, 3:4]))
         fill_plane(got_ion[o, 0:1], got_ion[o, 1:2], buf.at[:, pl.ds(0, slots)], buf.at[:, pl.ds(slots, slots)])
 
-    def add(buf, v):
-        acc[...] += sums_of(v, buf[:, :slots], buf[:, slots:])
+    def add(v, hi, lo):
+        acc[...] += mm(hi, v[...], NT)
+        acc[:, : 2 * L_ROWS] += mm(lo, v[: 2 * L_ROWS], NT)
 
     put(even_v, z * q)
     ion_copy(1).wait_recv()
-    acc[...] = sums_of(even_v, table[:WAVES, :slots], table[WAVES:, :slots])
+    acc[...] = jnp.zeros_like(acc)
+    add(even_v, table[:WAVES, :slots], table[WAVES:, :slots])
     take(1, odd, odd_v)
 
     hist_sib_copy().wait_recv()
@@ -338,9 +335,9 @@
         o = 2 * i + 2
         ion_copy(o).wait_recv()
         ion_copy(o + 1).wait_recv()
-        add(odd, odd_v)
+        add(odd_v, odd[:, :slots], odd[:, slots:])
         take(o, even, even_v)
-        add(even, even_v)
+        add(even_v, even[:, :slots], even[:, slots:])
         take(o + 1, odd, odd_v)
 
     if chips <= 8:
@@ -349,19 +346,21 @@
             for o in range(2, chips):
                 ion_copy(o).wait_recv()
             for o in range(2, chips, 2):
-                add(odd, odd_v)
+                add(odd_v, odd[:, :slots], odd[:, slots:])
                 take(o, even, even_v)
-                add(even, even_v)
+                add(even_v, even[:, :slots], even[:, slots:])
                 take(o + 1, odd, odd_v)
-            add(odd, odd_v)
+            add(odd_v, odd[:, :slots], odd[:, slots:])
 
         pl.loop(0, 1 + lax.div(blk, blks))(rest)
     else:
         pl.loop(0, chips // 2 - 1)(pair)
-        add(odd, odd_v)
-    for i in range(2 * L_ROWS // 8):
-        for t in range(W_TILES):
-            sums[i * W_TILES + t] = acc[8 * i : 8 * i + 8, 128 * t : 128 * t + 128]
+        add(odd_v, odd[:, :slots], odd[:, slots:])
+    for t in range(W_TILES):
+        value = acc[128 * t : 128 * t + 128].T
+        value = value[: 2 * L_ROWS] + value[2 * L_ROWS :]
+        for i in range(2 * L_ROWS // 8):
+            sums[i * W_TILES + t] = value[8 * i : 8 * i + 8]
     sums_copy().start()
 
     each(devices, lambda o: mail_copy(o).wait_recv())
@@ -525,7 +524,7 @@
             pltpu.VMEM((H_TILES, 8, 128), F32),
             pltpu.VMEM((H_TILES, 8, 128), F32),
             pltpu.VMEM((blks // 2, H_TILES, 8, 128), F32),
-            pltpu.VMEM((2 * L_ROWS, WAVES), F32),
+            pltpu.VMEM((WAVES, 4 * L_ROWS), F32),
             pltpu.VMEM((T_TILES, 8, 128), F32),
             pltpu.VMEM((T_TILES, 8, 128), F32),
             pltpu.VMEM((2 * L_ROWS, slots + atoms), F32),

time: 20.5 us -> 20.2 us (0.985)
  Pallas kernels: 17.8 us -> 17.5 us
    pallas_call x1, Pallas kernels: 17.8 us -> 17.5 us  [body(): pl.pallas_call(functools.partial(kernel, blks, rows, cap, scale), out_sha...]
where the time goes in v6:
time: 20.2 us; the launch traced here: 20 us
  Pallas kernels  17.5 us (87%)
  between operations  1.28 us (6%)
  local copies, waits for them, and re-layouts  1.2 us (6%)
    pallas_call x1, Pallas kernels, body(): pl.pallas_call(functools.partial(kernel, blks, rows, cap, scale), out_sha...  17.5 us
    unnamed x2, local copies, waits for them, and re-layouts  1.2 us

profile of v6, /device:TPU:0, one launch (start us, length us, event | category | flops | bytes accessed | tf_op | source)
XLA Modules:
  0.0 20.0 jit_solution(16885099908986882056)
XLA Ops:
  1.3 17.5 %shard_map.77 = (f32[3,768]{1,0:T(4,128)S(1)}, f32[3,512]{1,0:T(4,128)S(1)}) custom-call(f32[3,768]{1,0:T(4,128)} %coords_in.1, f32[768]{0:T(1024)} %charges_in.1, s32[1]{0:T(128)S(6)} %copy.12.counts_in, s32[768]{0:T(1024)} %send_in.1, s32[512]{0:T(512)} %recv_in.1, s32[3,6144]{1,0:T(4,128)} %wave_in.1), custom_call_target="tpu_custom_call" | custom-call | tf_op jit(solution)/shard_map/pallas_call | solution.py:509
  18.8 0.6 %copy.10 = f32[3,768]{1,0:T(4,128)} copy(f32[3,768]{1,0:T(4,128)S(1)} %get-tuple-element.2) | data formatting | bytes 18432
  19.4 0.6 %copy.11 = f32[3,512]{1,0:T(4,128)} copy(f32[3,512]{1,0:T(4,128)S(1)} %get-tuple-element.3) | data formatting | bytes 12288

commit v7 on v6

--- a/solution.py
+++ b/solution.py
@@ -266,7 +266,7 @@
 
     loads[4].wait()
     k_local = wave.shape[1]
-    part = 1536 if k_local % 1536 == 0 else k_local
+    part = 3072 if k_local % 3072 == 0 else k_local
     found[...] = jnp.zeros_like(found)
 
     def count(i):

time: 20.2 us -> 20 us (0.990)
    pallas_call x1, Pallas kernels: 17.5 us -> 17.3 us  [body(): pl.pallas_call(functools.partial(kernel, blks, rows, cap, scale), out_sha...]
where the time goes in v7:
time: 20 us; the launch traced here: 19.8 us
  Pallas kernels  17.3 us (86%)
  between operations  1.28 us (6%)
  local copies, waits for them, and re-layouts  1.2 us (6%)
    pallas_call x1, Pallas kernels, body(): pl.pallas_call(functools.partial(kernel, blks, rows, cap, scale), out_sha...  17.3 us
    unnamed x2, local copies, waits for them, and re-layouts  1.2 us

profile of v7, /device:TPU:0, one launch (start us, length us, event | category | flops | bytes accessed | tf_op | source)
XLA Modules:
  0.0 19.8 jit_solution(5452832012853134804)
XLA Ops:
  1.3 17.3 %shard_map.77 = (f32[3,768]{1,0:T(4,128)S(1)}, f32[3,512]{1,0:T(4,128)S(1)}) custom-call(f32[3,768]{1,0:T(4,128)} %coords_in.1, f32[768]{0:T(1024)} %charges_in.1, s32[1]{0:T(128)S(6)} %copy.12.counts_in, s32[768]{0:T(1024)} %send_in.1, s32[512]{0:T(512)} %recv_in.1, s32[3,6144]{1,0:T(4,128)} %wave_in.1), custom_call_target="tpu_custom_call" | custom-call | tf_op jit(solution)/shard_map/pallas_call | solution.py:509
  18.6 0.6 %copy.10 = f32[3,768]{1,0:T(4,128)} copy(f32[3,768]{1,0:T(4,128)S(1)} %get-tuple-element.2) | data formatting | bytes 18432
  19.2 0.6 %copy.11 = f32[3,512]{1,0:T(4,128)} copy(f32[3,512]{1,0:T(4,128)S(1)} %get-tuple-element.3) | data formatting | bytes 12288
